TPU v7x, 32 devices: a whole 2x2x4 slice. The times are simulated.
32 devices in a mesh: req: 8 (over y, x, core), blk: 4 (over z).
Axes of the slice: x: 2, y: 2, z: 4, core: 2. Of those that a mesh axis runs over, the one named last changes fastest.
Arguments:
- x_img: bfloat16 [8, 1024, 1536], P('req', 'blk'), may hold values from -0.3 to 0.3
- x_txt: bfloat16 [8, 154, 1536], P('req'), may hold values from -6 to 6
- modulation: float32 [8, 7, 1536], P('req'), may hold values from -8 to 8
- w_img: bfloat16 [1536, 2304], P(None, 'req'), may hold values from -0.375 to 0.375
- w_txt: bfloat16 [1536, 1536], P(None, 'req'), may hold values from -0.15625 to 0.15625
- w_out: bfloat16 [768, 1536], P('req'), may hold values from -0.21875 to 0.21875
- w_final: bfloat16 [1536, 64], replicated, may hold values from -0.15625 to 0.15625
- lengths: int32 [8], P('req'), may hold values from 16 to 154, as said below
- block_mask: int32 [8, 4, 4], P('req', 'blk'), may hold values from 0 to 1, as said below
- timestep: int32 [8], P('req'), may hold values from 0 to 27
- latent: float32 [8, 16, 32, 128], P('req', None, 'blk'), may hold values from -6 to 6
- conv_w: bfloat16 [512, 144], replicated, may hold values from -0.5 to 0.5
Outputs:
- velocity: float32 [8, 16, 32, 128], P('req', None, 'blk')
- latent_next: float32 [8, 16, 32, 128], P('req', None, 'blk')
- features: bfloat16 [8, 512, 32, 128], P('req', None, 'blk')
Inputs may be any that keep to these rules, and one draw needn't show every extreme that they name: Text keys from position lengths[r] on are padding; some request uses all 154 text tokens. Every tile may attend to its own keys: block_mask[r, t, t] = 1.
All inputs are finite; a program needn't handle non-finite values.
Results may differ from a plain program's by a relative error of at most 0.0063.
Values may be sent and summed in bfloat16 or wider, within the bound.
A program may use at most 192 MiB of HBM per device.

v0:
```python
import jax
import jax.numpy as jnp
from jax import lax
from jax.sharding import PartitionSpec as P

HD = 64
GRIDW = 64
PATCH = 2
LATC = 16
NSTEPS = 28
NORM_EPS = 1e-06
SHIFT_FACTOR = 3.0
LATENT_SCALE = 1.5305
LATENT_SHIFT = 0.0609
NEG_LARGE = -1e30
SCORE_SCALE = 0.125


def with_halo(block, sides, width):
    for axis, dim in sides:
        count = lax.axis_size(axis)
        forward = [(i, i + 1) for i in range(count - 1)]
        backward = [(target, source) for source, target in forward]
        low = lax.ppermute(
            lax.slice_in_dim(block, block.shape[dim] - width, None, axis=dim), axis, forward
        )
        high = lax.ppermute(lax.slice_in_dim(block, 0, width, axis=dim), axis, backward)
        block = jnp.concatenate([low, block, high], axis=dim)
    return block


def layer_norm(values):
    values = values.astype(jnp.float32)
    center = values - jnp.mean(values, axis=-1, keepdims=True)
    spread = jnp.mean(center * center, axis=-1, keepdims=True)
    return center * lax.rsqrt(spread + NORM_EPS)


def modulate(values, shift_row, scale_row):
    return layer_norm(values) * (1.0 + scale_row) + shift_row


def sigma_of(step_index, step_count):
    fraction = 1.0 - step_index.astype(jnp.float32) / step_count
    return SHIFT_FACTOR * fraction / (1.0 + (SHIFT_FACTOR - 1.0) * fraction)


def unpatchify(token_out, grid_width, patch_size, channels):
    patch_rows = token_out.shape[0] // grid_width
    shaped = token_out.reshape(patch_rows, grid_width, patch_size, patch_size, channels)
    shaped = jnp.transpose(shaped, (4, 0, 2, 1, 3))
    return shaped.reshape(channels, patch_rows * patch_size, grid_width * patch_size)


def convolve(padded, conv_w):
    row_count = padded.shape[1] - 2
    col_count = padded.shape[2] - 2
    tap_list = [
        padded[:, tap_row : tap_row + row_count, tap_col : tap_col + col_count]
        for tap_row in range(3)
        for tap_col in range(3)
    ]
    stacked = jnp.stack(tap_list, axis=1).reshape(padded.shape[0] * 9, row_count * col_count)
    convolved = jnp.dot(conv_w, stacked, preferred_element_type=jnp.float32)
    return convolved.reshape(conv_w.shape[0], row_count, col_count)


def text_state(queries, keys_txt, vals_txt, length):
    text_allowed = (jnp.arange(keys_txt.shape[0], dtype=jnp.int32) < length)[None, None, :]
    text_scores = (
        jnp.einsum("qhd,khd->qhk", queries, keys_txt, preferred_element_type=jnp.float32)
        * SCORE_SCALE
    )
    text_scores = jnp.where(text_allowed, text_scores, NEG_LARGE)
    text_max = jnp.max(text_scores, axis=2)
    text_weights = jnp.where(text_allowed, jnp.exp(text_scores - text_max[:, :, None]), 0.0)
    text_acc = jnp.einsum(
        "qhk,khd->qhd",
        text_weights.astype(jnp.bfloat16),
        vals_txt,
        preferred_element_type=jnp.float32,
    )
    return (text_max, jnp.sum(text_weights, axis=2), text_acc)


def absorb_block(previous, queries, head_keys, head_vals, allowed):
    old_max, old_sum, old_acc = previous
    scores = (
        jnp.einsum("qhd,khd->qhk", queries, head_keys, preferred_element_type=jnp.float32)
        * SCORE_SCALE
    )
    scores = jnp.where(allowed, scores, NEG_LARGE)
    new_max = jnp.maximum(old_max, jnp.max(scores, axis=2))
    weights = jnp.where(allowed, jnp.exp(scores - new_max[:, :, None]), 0.0)
    factor = jnp.exp(old_max - new_max)
    summed = jnp.einsum(
        "qhk,khd->qhd", weights.astype(jnp.bfloat16), head_vals, preferred_element_type=jnp.float32
    )
    return (
        new_max,
        old_sum * factor + jnp.sum(weights, axis=2),
        old_acc * factor[:, :, None] + summed,
    )


def absorb_maybe(previous, queries, head_keys, head_vals, allowed):
    return absorb_block(previous, queries, head_keys, head_vals, allowed)


def on_device(
    x_img,
    x_txt,
    modulation,
    w_img,
    w_txt,
    w_out,
    w_final,
    lengths,
    block_mask,
    timestep,
    latent,
    conv_w,
):
    tokens = x_img[0]
    factors = modulation[0]
    tok_rows = tokens.shape[0]
    head_cols = w_out.shape[0] * lax.axis_size("req")
    head_count = head_cols // HD
    h_img = modulate(tokens, factors[0], factors[1]).astype(jnp.bfloat16)
    h_txt = modulate(x_txt[0], factors[3], factors[4]).astype(jnp.bfloat16)
    qkv = jnp.dot(
        h_img, lax.all_gather(w_img, "req", axis=1, tiled=True), preferred_element_type=jnp.float32
    ).astype(jnp.bfloat16)
    kv_txt = jnp.dot(
        h_txt, lax.all_gather(w_txt, "req", axis=1, tiled=True), preferred_element_type=jnp.float32
    ).astype(jnp.bfloat16)
    keys_txt = kv_txt[:, :head_cols].reshape(-1, head_count, HD)
    vals_txt = kv_txt[:, head_cols:].reshape(-1, head_count, HD)
    length = lengths[0]
    queries = qkv[:, :head_cols].reshape(tok_rows, head_count, HD)
    keys_img = qkv[:, head_cols : 2 * head_cols]
    vals_img = qkv[:, 2 * head_cols :]
    mask_row = block_mask[0, 0]
    tile_count = mask_row.shape[0]
    start_state = text_state(queries, keys_txt, vals_txt, length)
    piece_keys = lax.all_gather(keys_img, "blk", axis=0, tiled=True)
    piece_vals = lax.all_gather(vals_img, "blk", axis=0, tiled=True)
    piece_len = piece_keys.shape[0]
    key_tile = jnp.arange(piece_len, dtype=jnp.int32) // tok_rows
    tile_hit = key_tile[:, None] == jnp.arange(tile_count, dtype=jnp.int32)[None, :]
    allowed = jnp.sum(jnp.where(tile_hit, mask_row[None, :], 0), axis=1) == 1
    head_keys = piece_keys.reshape(piece_len, head_count, HD)
    head_vals = piece_vals.reshape(piece_len, head_count, HD)
    run_max, run_sum, run_acc = absorb_maybe(
        start_state, queries, head_keys, head_vals, allowed[None, None, :]
    )
    attended = (run_acc / run_sum[:, :, None]).reshape(tok_rows, head_cols).astype(jnp.bfloat16)
    projected = jnp.dot(
        attended,
        lax.all_gather(w_out, "req", axis=0, tiled=True),
        preferred_element_type=jnp.float32,
    )
    residual = tokens.astype(jnp.float32) + factors[2] * projected
    final_in = modulate(residual, factors[5], factors[6]).astype(jnp.bfloat16)
    token_out = jnp.dot(final_in, w_final, preferred_element_type=jnp.float32)
    velocity = unpatchify(token_out, GRIDW, PATCH, LATC)[None]
    step_index = timestep[0]
    sigma_step = sigma_of(step_index + 1, NSTEPS) - sigma_of(step_index, NSTEPS)
    latent_next = latent + sigma_step * velocity
    decoded = (latent_next / LATENT_SCALE + LATENT_SHIFT).astype(jnp.bfloat16)
    padded = with_halo(decoded, (("blk", 2),), 1)
    padded = jnp.pad(padded[0], ((0, 0), (0, 0), (1, 1)))
    features = convolve(padded, conv_w).astype(jnp.bfloat16)[None]
    return (velocity, latent_next, features)


def solution(mesh):
    return jax.shard_map(
        on_device,
        mesh=mesh,
        in_specs=(
            P("req", "blk", None),
            P("req", None, None),
            P("req", None, None),
            P(None, "req"),
            P(None, "req"),
            P("req", None),
            P(),
            P("req"),
            P("req", "blk", None),
            P("req"),
            P("req", None, "blk", None),
            P(),
        ),
        out_specs=(
            P("req", None, "blk", None),
            P("req", None, "blk", None),
            P("req", None, "blk", None),
        ),
        check_vma=False,
    )
```

profile of v0, /device:TPU:0, one launch (start us, length us, event | category | flops | bytes accessed | tf_op | source)
XLA Modules:
  0.0 230.1 jit_solution(16971153236048344387)
XLA Ops:
  7.2 0.0 copy-start
  7.2 0.0 all-gather.8.cloned.1.call-start
  7.2 0.7 all-gather.8.cloned.1.call-update
  7.9 0.0 all-gather.6.cloned.1.call-start
  8.0 0.7 all-gather.6.cloned.1.call-update
  8.7 0.0 all-gather.10.cloned.1.call-start
  8.7 0.9 add_reduce_fusion
  9.6 0.0 copy-done.2
  9.6 0.2 convert_reduce_fusion
  9.8 0.3 fusion.14
  10.2 51.3 %all-gather.8.cloned.1.call-done = bf16[1536,2304]{0,1:T(8,128)(2,1)} async-done(((bf16[1536,288]{0,1:T(8,128)(2,1)}), bf16[1536,2304]{0,1:T(8,128)(2,1)}) %all-gather.8.cloned.1.call-update) | async-done | bytes 7077904 | tf_op jit(solution)/shard_map/all_gather | solution.py:132
  61.5 5.2 %convolution_convert_fusion = bf16[256,2304]{1,0:T(8,128)(2,1)S(1)} fusion(bf16[1536,2304]{0,1:T(8,128)(2,1)} %all-gather.8.cloned.1.call-done, bf16[1,256,1536]{2,1,0:T(8,128)(2,1)S(1)} %copy-done.2, f32[1536]{0:T(1024)S(1)} %get-tuple-element.16, f32[1536]{0:T(1024)S(1)} %get-tuple-element.17, f32[256]{0:T(256)S(1)} %add_rsqrt_fusion.1, ...), kind=kOutput, calls=%fused_computation.10 | convolution fusion | flops 1814888448 | bytes 9058304 | tf_op jit(solution)/shard_map/dot_general | solution.py:131
  66.7 0.0 copy-start.4
  66.7 0.0 copy-start.8
  66.7 0.0 copy-start.7
  66.7 1.0 fusion.69
  67.7 0.0 all-gather.10.cloned.1.call-update
  67.7 0.0 all-gather.12.cloned.1.call-start
  67.7 0.5 all-gather.12.cloned.1.call-update
  68.3 0.0 all-gather.14.cloned.1.call-start
  68.3 0.5 all-gather.14.cloned.1.call-update
  69.5 0.1 convert_reduce_fusion.1
  69.7 0.3 fusion.30
  70.7 0.0 copy-done.8
  70.7 0.1 select_reduce_fusion
  70.8 1.0 copy.66
  71.9 30.4 %all-gather.6.cloned.1.call-done = bf16[1536,1536]{0,1:T(8,128)(2,1)} async-done(((bf16[1536,192]{0,1:T(8,128)(2,1)}), bf16[1536,1536]{0,1:T(8,128)(2,1)}) %all-gather.6.cloned.1.call-update) | async-done | bytes 4718608 | tf_op jit(solution)/shard_map/all_gather | solution.py:135
  102.3 4.0 %convolution_convert_fusion.1 = bf16[154,1536]{1,0:T(8,128)(2,1)S(1)} fusion(bf16[1536,1536]{0,1:T(8,128)(2,1)} %all-gather.6.cloned.1.call-done, bf16[1,154,1536]{2,1,0:T(8,128)(2,1)S(1)} %copy-done.4, f32[1536]{0:T(1024)S(1)} %get-tuple-element.18, f32[1536]{0:T(1024)S(1)} %get-tuple-element.19, f32[154]{0:T(256)S(1)} %add_rsqrt_fusion.2, ...), kind=kOutput, calls=%fused_computation.13 | convolution fusion | flops 728318976 | bytes 5678288 | tf_op jit(solution)/shard_map/dot_general | solution.py:134
  106.4 0.9 copy.60
  107.3 0.9 copy.59
  108.3 0.2 copy.61
  108.4 1.6 bitcast_reduce_fusion.1
  110.0 0.6 fusion.18
  110.6 30.5 %all-gather.10.cloned.1.call-done = bf16[1024,768]{1,0:T(8,128)(2,1)} async-done(((bf16[256,768]{1,0:T(8,128)(2,1)}), bf16[1024,768]{1,0:T(8,128)(2,1)}) %all-gather.10.cloned.1.call-update) | async-done | bytes 1572880 | tf_op jit(solution)/shard_map/all_gather | solution.py:146
  141.0 2.6 %copy.62 = bf16[1024,768]{0,1:T(8,128)(2,1)} copy(bf16[1024,768]{1,0:T(8,128)(2,1)} %all-gather.10.cloned.1.call-done) | data formatting | bytes 3145728 | tf_op jit(solution)/shard_map/all_gather | solution.py:146
  143.6 8.8 %bitcast_reduce_fusion = (f32[256,12]{0,1:T(8,128)S(1)}, f32[12,1024,256]{2,1,0:T(8,128)}) fusion(pred[1024]{0:T(1024)(128)(4,1)S(1)} %broadcast_compare_fusion, bf16[1024,12,64]{0,2,1:T(8,128)(2,1)} %bitcast.129, bf16[256,12,64]{0,2,1:T(8,128)(2,1)S(1)} %bitcast.134), kind=kOutput, calls=%fused_computation.1 | convolution fusion | flops 412087296 | bytes 14562304 | tf_op jit(solution)/shard_map/qhd,khd->qhk/dot_general | solution.py:89
  152.5 26.0 %all-gather.12.cloned.1.call-done = bf16[1024,768]{1,0:T(8,128)(2,1)} async-done(((bf16[256,768]{1,0:T(8,128)(2,1)}), bf16[1024,768]{1,0:T(8,128)(2,1)}) %all-gather.12.cloned.1.call-update) | async-done | bytes 1572880 | tf_op jit(solution)/shard_map/all_gather | solution.py:147
  178.4 2.6 %copy.63 = bf16[1024,768]{0,1:T(8,128)(2,1)} copy(bf16[1024,768]{1,0:T(8,128)(2,1)} %all-gather.12.cloned.1.call-done) | data formatting | bytes 3145728 | tf_op jit(solution)/shard_map/all_gather | solution.py:147
  181.0 7.2 %fusion.2 = f32[256,12]{0,1:T(8,128)S(1)} fusion(f32[12,1024,256]{2,1,0:T(8,128)} %get-tuple-element.45, f32[256,12]{0,1:T(8,128)S(1)} %max.13, pred[1024]{0:T(1024)(128)(4,1)S(1)} %broadcast_compare_fusion), kind=kLoop, calls=%fused_computation.5 | loop fusion | flops 15725568 | bytes 12608512 | tf_op jit(solution)/shard_map/reduce_sum | solution.py:101
  188.3 1.3 copy-done.1
  189.6 4.3 %fusion.20 = f32[256,12,64]{0,2,1:T(8,128)S(1)} fusion(bf16[1024,12,64]{0,2,1:T(8,128)(2,1)} %bitcast.135, f32[12,1024,256]{2,1,0:T(8,128)S(1)} %copy-done.1, f32[256,12]{0,1:T(8,128)S(1)} %max.13, pred[1024]{0:T(1024)(128)(4,1)S(1)} %broadcast_compare_fusion), kind=kOutput, calls=%fused_computation.33 | convolution fusion | flops 418381824 | bytes 14955520 | tf_op jit(solution)/shard_map/qhk,khd->qhd/dot_general | solution.py:96
  193.9 0.0 copy-done.5
  193.9 0.7 fusion.26
  194.6 13.5 %all-gather.14.cloned.1.call-done = bf16[768,1536]{1,0:T(8,128)(2,1)} async-done(((bf16[96,1536]{1,0:T(8,128)(2,1)}), bf16[768,1536]{1,0:T(8,128)(2,1)}) %all-gather.14.cloned.1.call-update) | async-done | bytes 2359312 | tf_op jit(solution)/shard_map/all_gather | solution.py:160
  208.1 2.5 %fusion.72 = (f32[256]{0:T(256)S(1)}, f32[256,1536]{1,0:T(8,128)S(1)}) fusion(bf16[256,768]{0,1:T(8,128)(2,1)S(1)} %bitcast.137, bf16[768,1536]{1,0:T(8,128)(2,1)} %all-gather.14.cloned.1.call-done, f32[1536]{0:T(1024)S(1)} %get-tuple-element.20, bf16[1,256,1536]{2,1,0:T(8,128)(2,1)S(1)} %copy-done.2), kind=kOutput, calls=%fused_computation.127 | convolution fusion | flops 605552384 | bytes 5118976 | tf_op jit(solution)/shard_map/dot_general | solution.py:158
  210.6 0.0 copy-start.3
  210.6 0.3 multiply_reduce_fusion
  211.0 0.5 fusion.46
  211.4 0.1 reshape.190
  211.6 0.3 copy.65
  211.8 0.0 copy-start.6
  211.9 0.1 add_convert_fusion.2
  212.0 3.4 %collective-permute-start = (bf16[1,16,1,128]{1,3,2,0:T(8,128)(2,1)S(1)}, bf16[1,16,1,128]{1,3,2,0:T(8,128)(2,1)S(1)}, u32[]{:S(2)}, u32[]{:S(2)}) collective-permute-start(bf16[1,16,1,128]{1,3,2,0:T(8,128)(2,1)S(1)} %get-tuple-element.31), channel_id=1, source_target_pairs={{0,1},{1,2},{2,3},{4,5},{5,6},{6,7},{8,9},{9,10},{10,11},{12,13},{... | collective-permute-start | bytes 12296 | tf_op jit(solution)/shard_map/ppermute | solution.py:24
  215.4 1.3 collective-permute-start.1
  216.7 0.1 copy.68
  216.8 0.8 copy.79
  217.6 0.8 copy.80
  218.4 0.0 collective-permute-done
  218.4 0.1 copy.67
  218.5 2.7 %collective-permute-done.1 = bf16[1,16,1,128]{1,3,2,0:T(8,128)(2,1)S(1)} collective-permute-done((bf16[1,16,1,128]{1,3,2,0:T(8,128)(2,1)S(1)}, bf16[1,16,1,128]{1,3,2,0:T(8,128)(2,1)S(1)}, u32[]{:S(2)}, u32[]{:S(2)}) %collective-permute-start.1) | collective-permute-done | bytes 4128 | tf_op jit(solution)/shard_map/ppermute | solution.py:27
  221.2 0.1 copy.69
  221.3 0.1 fusion.59
  221.6 0.5 convolution_convert_fusion.2
  222.1 1.5 copy.81
  (31 shorter events, 0.3 us)
Async XLA Ops:
  7.2 203.8 %copy-start = (bf16[1536,64]{0,1:T(8,128)(2,1)S(1)}, bf16[1536,64]{0,1:T(8,128)(2,1)}, u32[]{:S(2)}) copy-start(bf16[1536,64]{0,1:T(8,128)(2,1)} %param.18) | copy-start | bytes 589828
  7.2 2.5 %copy-start.2 = (bf16[1,256,1536]{2,1,0:T(8,128)(2,1)S(1)}, bf16[1,256,1536]{2,1,0:T(8,128)(2,1)}, u32[]{:S(2)}) copy-start(bf16[1,256,1536]{2,1,0:T(8,128)(2,1)} %param.12) | copy-start | bytes 2359300
  7.2 54.3 %all-gather.8.cloned.1.call-start = ((), (), s32[]{:S(2)}) async-start(), calls=%async_computation.1 | async-start | bytes 7962624 | tf_op jit(solution)/shard_map/all_gather | solution.py:132
  7.9 94.4 %all-gather.6.cloned.1.call-start = ((), (), s32[]{:S(2)}) async-start(), calls=%async_computation | async-start | bytes 5308416 | tf_op jit(solution)/shard_map/all_gather | solution.py:135
  8.7 132.4 %all-gather.10.cloned.1.call-start = ((), (), s32[]{:S(2)}) async-start(), calls=%async_computation.2 | async-start | bytes 1966080 | tf_op jit(solution)/shard_map/all_gather | solution.py:146
  66.7 2.9 %copy-start.4 = (bf16[1,154,1536]{2,1,0:T(8,128)(2,1)S(1)}, bf16[1,154,1536]{2,1,0:T(8,128)(2,1)}, u32[]{:S(2)}) copy-start(bf16[1,154,1536]{2,1,0:T(8,128)(2,1)} %param.13) | copy-start | bytes 1419268
  66.7 4.0 %copy-start.8 = (s32[1,1,4]{2,1,0:T(1,128)S(1)}, s32[1,1,4]{2,1,0:T(1,128)}, u32[]{:S(2)}) copy-start(s32[1,1,4]{2,1,0:T(1,128)} %param.20) | copy-start | bytes 52
  66.7 4.1 %copy-start.7 = (f32[1,16,8,128]{3,2,1,0:T(8,128)S(1)}, f32[1,16,8,128]{3,2,1,0:T(8,128)}, u32[]{:S(2)}) copy-start(f32[1,16,8,128]{3,2,1,0:T(8,128)} %param.22) | copy-start | bytes 196612
  67.7 110.8 %all-gather.12.cloned.1.call-start = ((), (), s32[]{:S(2)}) async-start(), calls=%async_computation.3 | async-start | bytes 1966080 | tf_op jit(solution)/shard_map/all_gather | solution.py:147
  68.3 139.8 %all-gather.14.cloned.1.call-start = ((), (), s32[]{:S(2)}) async-start(), calls=%async_computation.4 | async-start | bytes 2654208 | tf_op jit(solution)/shard_map/all_gather | solution.py:160
  181.0 8.5 %copy-start.1 = (f32[12,1024,256]{2,1,0:T(8,128)S(1)}, f32[12,1024,256]{2,1,0:T(8,128)}, u32[]{:S(2)}) copy-start(f32[12,1024,256]{2,1,0:T(8,128)} %get-tuple-element.45) | copy-start | bytes 37748740
  189.6 4.3 %copy-start.5 = (bf16[154,768]{0,1:T(8,128)(2,1)S(1)}, bf16[154,768]{0,1:T(8,128)(2,1)}, u32[]{:S(2)}) copy-start(bf16[154,768]{0,1:T(8,128)(2,1)} %copy.59) | copy-start | bytes 709636
  210.6 1.2 copy-start.3
  211.8 9.8 %copy-start.6 = (bf16[512,144]{0,1:T(8,128)(2,1)S(1)}, bf16[512,144]{0,1:T(8,128)(2,1)}, u32[]{:S(2)}) copy-start(bf16[512,144]{0,1:T(8,128)(2,1)} %param.23) | copy-start | bytes 442372
  212.0 6.4 %collective-permute-start = (bf16[1,16,1,128]{1,3,2,0:T(8,128)(2,1)S(1)}, bf16[1,16,1,128]{1,3,2,0:T(8,128)(2,1)S(1)}, u32[]{:S(2)}, u32[]{:S(2)}) collective-permute-start(bf16[1,16,1,128]{1,3,2,0:T(8,128)(2,1)S(1)} %get-tuple-element.31), channel_id=1, source_target_pairs={{0,1},{1,2},{2,3},{4,5},{5,6},{6,7},{8,9},{9,10},{10,11},{12,13},{... | collective-permute-start | bytes 12296 | tf_op jit(solution)/shard_map/ppermute | solution.py:24
  215.4 5.8 %collective-permute-start.1 = (bf16[1,16,1,128]{1,3,2,0:T(8,128)(2,1)S(1)}, bf16[1,16,1,128]{1,3,2,0:T(8,128)(2,1)S(1)}, u32[]{:S(2)}, u32[]{:S(2)}) collective-permute-start(bf16[1,16,1,128]{1,3,2,0:T(8,128)(2,1)S(1)} %get-tuple-element.32), channel_id=1, source_target_pairs={{1,0},{2,1},{3,2},{5,4},{6,5},{7,6},{9,8},{10,9},{11,10},{13,12},{... | collective-permute-start | bytes 12296 | tf_op jit(solution)/shard_map/ppermute | solution.py:27
Sparse Core Ops, SparseCore 0:
  9.9 51.5 all-gather.7
  63.4 38.9 all-gather.5
  103.9 37.0 all-gather.9
  142.5 35.9 all-gather.11
  180.2 27.8 all-gather.13
where the time goes:
time: 231 us; the launch traced here: 230 us
  waiting for transfers between devices  157 us (68%)
  matrix products  28 us (12%)
  between operations  15.5 us (7%)
  local copies, waits for them, and re-layouts  14.5 us (6%)
  other arithmetic  10.2 us (4%)
  starting transfers between devices  4.88 us (2%)
    all_gather x1, waiting for transfers between devices, on_device(): lax.all_gather(w_img, 'req', axis=1, tiled=True)  51.3 us
    all_gather x1, waiting for transfers between devices, on_device(): piece_keys = lax.all_gather(keys_img, 'blk', axis=0, tiled=True)  30.5 us
    all_gather x1, waiting for transfers between devices, on_device(): lax.all_gather(w_txt, 'req', axis=1, tiled=True)  30.4 us
    all_gather x1, waiting for transfers between devices, on_device(): piece_vals = lax.all_gather(vals_img, 'blk', axis=0, tiled=True)  26 us
    all_gather x1, waiting for transfers between devices, on_device(): lax.all_gather(w_out, 'req', axis=0, tiled=True)  13.5 us
    dot_general x1, matrix products, absorb_block(): jnp.einsum('qhd,khd->qhk', queries, head_keys, preferred_element_type=jnp...  8.82 us
    reduce_sum x1, other arithmetic, absorb_block(): jnp.sum(weights, axis=2)  7.21 us
    unnamed x30, local copies, waits for them, and re-layouts  5.57 us
  transfers between devices with their start and end apart: 7, of which 6 were waited for; matrix products, arithmetic and copies ran while one was open for 20% of the time, Pallas kernels for 0%

commit v1 on v0

--- a/solution.py
+++ b/solution.py
@@ -14,6 +14,18 @@
 LATENT_SHIFT = 0.0609
 NEG_LARGE = -1e30
 SCORE_SCALE = 0.125
+
+
+def doubled_up(x, axis, dim):
+    ways, here = (lax.axis_size(axis), lax.axis_index(axis))
+    grown, reach = (x, 1)
+    while reach < ways:
+        theirs = lax.ppermute(grown, axis, [(d, d ^ reach) for d in range(ways)])
+        mine_first = jnp.concatenate([grown, theirs], axis=dim)
+        theirs_first = jnp.concatenate([theirs, grown], axis=dim)
+        grown = jnp.where(here & reach == 0, mine_first, theirs_first)
+        reach = 2 * reach
+    return grown
 
 
 def with_halo(block, sides, width):
@@ -131,9 +143,9 @@
     qkv = jnp.dot(
         h_img, lax.all_gather(w_img, "req", axis=1, tiled=True), preferred_element_type=jnp.float32
     ).astype(jnp.bfloat16)
-    kv_txt = jnp.dot(
-        h_txt, lax.all_gather(w_txt, "req", axis=1, tiled=True), preferred_element_type=jnp.float32
-    ).astype(jnp.bfloat16)
+    kv_txt = jnp.dot(h_txt, doubled_up(w_txt, "req", 1), preferred_element_type=jnp.float32).astype(
+        jnp.bfloat16
+    )
     keys_txt = kv_txt[:, :head_cols].reshape(-1, head_count, HD)
     vals_txt = kv_txt[:, head_cols:].reshape(-1, head_count, HD)
     length = lengths[0]

time: 231 us -> 218 us (0.944)
  waiting for transfers between devices: 157 us -> 135 us
  other arithmetic: 10.2 us -> 16 us
  starting transfers between devices: 4.88 us -> 7.81 us
    ppermute x0 -> x3, waiting for transfers between devices: none -> 80.4 us  [doubled_up(): theirs = lax.ppermute(grown, axis, [(d, d ^ reach) for d in range(ways)])]
    all_gather x1, waiting for transfers between devices: 30.5 us -> 0.02 us  [on_device(): piece_keys = lax.all_gather(keys_img, 'blk', axis=0, tiled=True)]
    all_gather x1 -> x0, waiting for transfers between devices: 30.4 us -> none  [on_device(): lax.all_gather(w_txt, 'req', axis=1, tiled=True)]
    all_gather x1, waiting for transfers between devices: 26 us -> 0.01 us  [on_device(): piece_vals = lax.all_gather(vals_img, 'blk', axis=0, tiled=True)]
    all_gather x1, waiting for transfers between devices: 13.5 us -> 0.02 us  [on_device(): lax.all_gather(w_out, 'req', axis=0, tiled=True)]
    select_n x0 -> x2, other arithmetic: none -> 4.63 us  [doubled_up(): grown = jnp.where(here & reach == 0, mine_first, theirs_first)]
    ppermute x0 -> x3, starting transfers between devices: none -> 2.96 us  [doubled_up(): theirs = lax.ppermute(grown, axis, [(d, d ^ reach) for d in range(ways)])]
    unnamed x30 -> x34, local copies, waits for them, and re-layouts: 5.57 us -> 5.51 us
  transfers between devices with their start and end apart: 7 -> 9, of which waited for: 6 -> 5; matrix products, arithmetic and copies ran while one was open for 20% -> 21% of each run, Pallas kernels for 0% -> 0%
where the time goes in v1:
time: 218 us
  waiting for transfers between devices  135 us (62%)
  matrix products  28.9 us (13%)
  other arithmetic  16 us (7%)
  between operations  15.6 us (7%)
  local copies, waits for them, and re-layouts  14.6 us (7%)
  starting transfers between devices  7.81 us (4%)
    ppermute x3, waiting for transfers between devices, doubled_up(): theirs = lax.ppermute(grown, axis, [(d, d ^ reach) for d in range(ways)])  80.4 us
    all_gather x1, waiting for transfers between devices, on_device(): lax.all_gather(w_img, 'req', axis=1, tiled=True)  50.9 us
    dot_general x1, matrix products, absorb_block(): jnp.einsum('qhd,khd->qhk', queries, head_keys, preferred_element_type=jnp...  8.82 us
    reduce_sum x1, other arithmetic, absorb_block(): jnp.sum(weights, axis=2)  7.2 us
    unnamed x34, local copies, waits for them, and re-layouts  5.51 us
    dot_general x1, matrix products, on_device(): jnp.dot(h_img, lax.all_gather(w_img, 'req', axis=1, tiled=True), preferre...  5.16 us
    dot_general x1, matrix products, on_device(): jnp.dot(h_txt, doubled_up(w_txt, 'req', 1), preferred_element_type=jnp.fl...  4.91 us
    select_n x2, other arithmetic, doubled_up(): grown = jnp.where(here & reach == 0, mine_first, theirs_first)  4.63 us
  transfers between devices with their start and end apart: 9, of which 5 were waited for; matrix products, arithmetic and copies ran while one was open for 21% of the time, Pallas kernels for 0%

profile of v1, /device:TPU:0, one launch (start us, length us, event | category | flops | bytes accessed | tf_op | source)
XLA Modules:
  0.0 217.7 jit_solution(1076830871783930899)
XLA Ops:
  7.2 0.0 copy-start
  7.2 0.0 copy-start.2
  7.2 0.0 all-gather.5.cloned.1.call-start
  7.2 0.7 all-gather.5.cloned.1.call-update
  7.9 0.0 all-gather.7.cloned.1.call-start
  8.0 0.9 add_reduce_fusion
  8.9 1.3 convert_reduce_fusion
  10.2 0.3 fusion.22
  10.6 50.9 %all-gather.5.cloned.1.call-done = bf16[1536,2304]{0,1:T(8,128)(2,1)} async-done(((bf16[1536,288]{0,1:T(8,128)(2,1)}), bf16[1536,2304]{0,1:T(8,128)(2,1)}) %all-gather.5.cloned.1.call-update) | async-done | bytes 7077904 | tf_op jit(solution)/shard_map/all_gather | solution.py:144
  61.5 5.2 %convolution_convert_fusion = bf16[256,2304]{1,0:T(8,128)(2,1)S(1)} fusion(bf16[1536,2304]{0,1:T(8,128)(2,1)} %all-gather.5.cloned.1.call-done, bf16[1,256,1536]{2,1,0:T(8,128)(2,1)S(1)} %copy-done.2, f32[1536]{0:T(1024)S(1)} %get-tuple-element.16, f32[1536]{0:T(1024)S(1)} %get-tuple-element.17, f32[256]{0:T(256)S(1)} %add_rsqrt_fusion.1, ...), kind=kOutput, calls=%fused_computation.18 | convolution fusion | flops 1814888448 | bytes 9058304 | tf_op jit(solution)/shard_map/dot_general | solution.py:143
  66.7 0.0 copy-start.6
  66.7 1.1 fusion.78
  67.7 0.0 all-gather.7.cloned.1.call-update
  67.8 0.0 all-gather.9.cloned.1.call-start
  67.8 0.2 copy-done.6
  68.0 0.3 collective-permute-start
  68.3 1.9 collective-permute-done
  70.2 1.7 maximum_select_fusion.5
  71.8 1.5 collective-permute-start.1
  73.4 0.0 all-gather.9.cloned.1.call-update
  73.4 0.0 all-gather.11.cloned.1.call-start
  73.5 0.0 copy-start.4
  73.5 26.7 %collective-permute-done.1 = bf16[1536,384]{0,1:T(8,128)(2,1)} collective-permute-done((bf16[1536,384]{0,1:T(8,128)(2,1)S(1)}, bf16[1536,384]{0,1:T(8,128)(2,1)}, u32[]{:S(2)}, u32[]{:S(2)}) %collective-permute-start.1) | collective-permute-done | bytes 1179680 | tf_op jit(solution)/shard_map/ppermute | solution.py:23
  100.1 3.0 %maximum_select_fusion.4 = bf16[1536,768]{0,1:T(8,128)(2,1)} fusion(bf16[1536,384]{0,1:T(8,128)(2,1)} %collective-permute-done.1, bf16[1536,384]{0,1:T(8,128)(2,1)S(1)} %maximum_select_fusion.5, pred[]{:T(512)S(6)} %eq.31), kind=kLoop, calls=%fused_computation.22 | loop fusion | flops 10616832 | bytes 4718593 | tf_op jit(solution)/shard_map/jit(_where)/select_n | solution.py:26
  103.1 1.2 collective-permute-start.2
  104.3 0.0 all-gather.11.cloned.1.call-update
  105.6 1.0 copy.66
  106.8 0.1 select_reduce_fusion
  106.9 0.1 convert_reduce_fusion.1
  107.0 0.3 fusion.38
  107.3 51.9 %collective-permute-done.2 = bf16[1536,768]{0,1:T(8,128)(2,1)} collective-permute-done((bf16[1536,768]{0,1:T(8,128)(2,1)}, bf16[1536,768]{0,1:T(8,128)(2,1)}, u32[]{:S(2)}, u32[]{:S(2)}) %collective-permute-start.2) | collective-permute-done | bytes 2359328 | tf_op jit(solution)/shard_map/ppermute | solution.py:23
  159.2 4.9 %fusion.16 = bf16[154,1536]{1,0:T(8,128)(2,1)S(1)} fusion(bf16[1536,768]{0,1:T(8,128)(2,1)} %collective-permute-done.2, bf16[1536,768]{0,1:T(8,128)(2,1)} %maximum_select_fusion.4, pred[]{:T(512)S(6)} %eq.30, bf16[1,154,1536]{2,1,0:T(8,128)(2,1)S(1)} %copy-done.4, f32[1536]{0:T(1024)S(1)} %get-tuple-element.18, f32[1536]{0:T(1024)S(1)} %get-tuple-element.19, ...), kind=kOutput, calls=%fused_computation.21 | convolution fusion | flops 749552640 | bytes 5678289 | tf_op jit(solution)/shard_map/dot_general | solution.py:146
  164.2 0.9 copy.60
  165.1 0.9 copy.59
  166.0 0.2 copy.61
  166.2 1.6 bitcast_reduce_fusion.1
  167.8 0.6 fusion.26
  168.3 0.0 all-gather.7.cloned.1.call-done
  168.3 2.6 %copy.62 = bf16[1024,768]{0,1:T(8,128)(2,1)} copy(bf16[1024,768]{1,0:T(8,128)(2,1)} %all-gather.7.cloned.1.call-done) | data formatting | bytes 3145728 | tf_op jit(solution)/shard_map/all_gather | solution.py:158
  171.0 8.8 %bitcast_reduce_fusion = (f32[256,12]{0,1:T(8,128)S(1)}, f32[12,1024,256]{2,1,0:T(8,128)}) fusion(pred[1024]{0:T(1024)(128)(4,1)S(1)} %broadcast_compare_fusion, bf16[1024,12,64]{0,2,1:T(8,128)(2,1)} %bitcast.128, bf16[256,12,64]{0,2,1:T(8,128)(2,1)S(1)} %bitcast.133), kind=kOutput, calls=%fused_computation.1 | convolution fusion | flops 412087296 | bytes 14562304 | tf_op jit(solution)/shard_map/qhd,khd->qhk/dot_general | solution.py:101
  179.8 2.6 %copy.63 = bf16[1024,768]{0,1:T(8,128)(2,1)} copy(bf16[1024,768]{1,0:T(8,128)(2,1)} %all-gather.9.cloned.1.call-done) | data formatting | bytes 3145728 | tf_op jit(solution)/shard_map/all_gather | solution.py:159
  182.4 7.2 %fusion.2 = f32[256,12]{0,1:T(8,128)S(1)} fusion(f32[12,1024,256]{2,1,0:T(8,128)} %get-tuple-element.45, f32[256,12]{0,1:T(8,128)S(1)} %max.13, pred[1024]{0:T(1024)(128)(4,1)S(1)} %broadcast_compare_fusion), kind=kLoop, calls=%fused_computation.5 | loop fusion | flops 15725568 | bytes 12608512 | tf_op jit(solution)/shard_map/reduce_sum | solution.py:113
  189.6 1.0 copy-done.1
  190.6 4.3 %fusion.28 = f32[256,12,64]{0,2,1:T(8,128)S(1)} fusion(bf16[1024,12,64]{0,2,1:T(8,128)(2,1)} %bitcast.134, f32[12,1024,256]{2,1,0:T(8,128)S(1)} %copy-done.1, f32[256,12]{0,1:T(8,128)S(1)} %max.13, pred[1024]{0:T(1024)(128)(4,1)S(1)} %broadcast_compare_fusion), kind=kOutput, calls=%fused_computation.42 | convolution fusion | flops 418381824 | bytes 14955520 | tf_op jit(solution)/shard_map/qhk,khd->qhd/dot_general | solution.py:108
  194.9 0.7 fusion.34
  195.6 0.0 all-gather.11.cloned.1.call-done
  195.6 2.5 %fusion.81 = (f32[256]{0:T(256)S(1)}, f32[256,1536]{1,0:T(8,128)S(1)}) fusion(bf16[256,768]{0,1:T(8,128)(2,1)S(1)} %bitcast.136, bf16[768,1536]{1,0:T(8,128)(2,1)} %all-gather.11.cloned.1.call-done, f32[1536]{0:T(1024)S(1)} %get-tuple-element.20, bf16[1,256,1536]{2,1,0:T(8,128)(2,1)S(1)} %copy-done.2), kind=kOutput, calls=%fused_computation.138 | convolution fusion | flops 605552384 | bytes 5118976 | tf_op jit(solution)/shard_map/dot_general | solution.py:170
  198.2 0.0 copy-start.3
  198.2 0.3 multiply_reduce_fusion
  198.5 0.5 fusion.54
  199.0 0.1 reshape.190
  199.1 0.3 copy.65
  199.4 0.1 add_convert_fusion.2
  199.5 3.4 %collective-permute-start.3 = (bf16[1,16,1,128]{1,3,2,0:T(8,128)(2,1)S(1)}, bf16[1,16,1,128]{1,3,2,0:T(8,128)(2,1)S(1)}, u32[]{:S(2)}, u32[]{:S(2)}) collective-permute-start(bf16[1,16,1,128]{1,3,2,0:T(8,128)(2,1)S(1)} %get-tuple-element.31), channel_id=1, source_target_pairs={{0,1},{1,2},{2,3},{4,5},{5,6},{6,7},{8,9},{9,10},{10,11},{12,13},{... | collective-permute-start | bytes 12296 | tf_op jit(solution)/shard_map/ppermute | solution.py:36
  202.9 1.3 collective-permute-start.4
  204.2 0.1 copy.68
  204.3 0.8 copy.79
  205.2 0.8 copy.80
  206.0 0.1 copy.67
  206.0 2.7 %collective-permute-done.4 = bf16[1,16,1,128]{1,3,2,0:T(8,128)(2,1)S(1)} collective-permute-done((bf16[1,16,1,128]{1,3,2,0:T(8,128)(2,1)S(1)}, bf16[1,16,1,128]{1,3,2,0:T(8,128)(2,1)S(1)}, u32[]{:S(2)}, u32[]{:S(2)}) %collective-permute-start.4) | collective-permute-done | bytes 4128 | tf_op jit(solution)/shard_map/ppermute | solution.py:39
  208.7 0.1 copy.69
  208.8 0.1 fusion.67
  209.2 0.5 convolution_convert_fusion.1
  209.7 1.5 copy.81
  (40 shorter events, 0.3 us)
Async XLA Ops:
  7.2 191.3 %copy-start = (bf16[1536,64]{0,1:T(8,128)(2,1)S(1)}, bf16[1536,64]{0,1:T(8,128)(2,1)}, u32[]{:S(2)}) copy-start(bf16[1536,64]{0,1:T(8,128)(2,1)} %param.18) | copy-start | bytes 589828
  7.2 3.0 %copy-start.2 = (bf16[1,256,1536]{2,1,0:T(8,128)(2,1)S(1)}, bf16[1,256,1536]{2,1,0:T(8,128)(2,1)}, u32[]{:S(2)}) copy-start(bf16[1,256,1536]{2,1,0:T(8,128)(2,1)} %param.12) | copy-start | bytes 2359300
  7.2 54.3 %all-gather.5.cloned.1.call-start = ((), (), s32[]{:S(2)}) async-start(), calls=%async_computation | async-start | bytes 7962624 | tf_op jit(solution)/shard_map/all_gather | solution.py:144
  7.9 160.4 %all-gather.7.cloned.1.call-start = ((), (), s32[]{:S(2)}) async-start(), calls=%async_computation.1 | async-start | bytes 1966080 | tf_op jit(solution)/shard_map/all_gather | solution.py:158
  66.7 1.4 copy-start.6
  67.8 112.1 %all-gather.9.cloned.1.call-start = ((), (), s32[]{:S(2)}) async-start(), calls=%async_computation.2 | async-start | bytes 1966080 | tf_op jit(solution)/shard_map/all_gather | solution.py:159
  68.0 2.1 collective-permute-start
  71.8 28.3 %collective-permute-start.1 = (bf16[1536,384]{0,1:T(8,128)(2,1)S(1)}, bf16[1536,384]{0,1:T(8,128)(2,1)}, u32[]{:S(2)}, u32[]{:S(2)}) collective-permute-start(bf16[1536,384]{0,1:T(8,128)(2,1)S(1)} %maximum_select_fusion.5), channel_id=1, source_target_pairs={{0,8},{4,12},{8,0},{12,4},{16,24},{20,28},{24,16},{28,20},{1,9},{5... | collective-permute-start | bytes 3538952 | tf_op jit(solution)/shard_map/ppermute | solution.py:23
  73.4 122.2 %all-gather.11.cloned.1.call-start = ((), (), s32[]{:S(2)}) async-start(), calls=%async_computation.3 | async-start | bytes 2654208 | tf_op jit(solution)/shard_map/all_gather | solution.py:172
  73.4 32.2 %copy-start.9 = (f32[1,16,8,128]{3,2,1,0:T(8,128)S(1)}, f32[1,16,8,128]{3,2,1,0:T(8,128)}, u32[]{:S(2)}) copy-start(f32[1,16,8,128]{3,2,1,0:T(8,128)} %param.22) | copy-start | bytes 196612
  73.5 33.3 %copy-start.10 = (s32[1,1,4]{2,1,0:T(1,128)S(1)}, s32[1,1,4]{2,1,0:T(1,128)}, u32[]{:S(2)}) copy-start(s32[1,1,4]{2,1,0:T(1,128)} %param.20) | copy-start | bytes 52
  73.5 33.4 %copy-start.4 = (bf16[1,154,1536]{2,1,0:T(8,128)(2,1)S(1)}, bf16[1,154,1536]{2,1,0:T(8,128)(2,1)}, u32[]{:S(2)}) copy-start(bf16[1,154,1536]{2,1,0:T(8,128)(2,1)} %param.13) | copy-start | bytes 1419268
  103.1 56.1 %collective-permute-start.2 = (bf16[1536,768]{0,1:T(8,128)(2,1)}, bf16[1536,768]{0,1:T(8,128)(2,1)}, u32[]{:S(2)}, u32[]{:S(2)}) collective-permute-start(bf16[1536,768]{0,1:T(8,128)(2,1)} %maximum_select_fusion.4), channel_id=1, source_target_pairs={{0,16},{4,20},{8,24},{12,28},{16,0},{20,4},{24,8},{28,12},{1,17},{... | collective-permute-start | bytes 7077896 | tf_op jit(solution)/shard_map/ppermute | solution.py:23
  164.1 1.9 copy-start.5
  182.4 8.2 %copy-start.1 = (f32[12,1024,256]{2,1,0:T(8,128)S(1)}, f32[12,1024,256]{2,1,0:T(8,128)}, u32[]{:S(2)}) copy-start(f32[12,1024,256]{2,1,0:T(8,128)} %get-tuple-element.45) | copy-start | bytes 37748740
  190.6 4.3 %copy-start.7 = (bf16[154,768]{0,1:T(8,128)(2,1)S(1)}, bf16[154,768]{0,1:T(8,128)(2,1)}, u32[]{:S(2)}) copy-start(bf16[154,768]{0,1:T(8,128)(2,1)} %copy.59) | copy-start | bytes 709636
  198.2 1.2 copy-start.3
  199.4 9.8 %copy-start.8 = (bf16[512,144]{0,1:T(8,128)(2,1)S(1)}, bf16[512,144]{0,1:T(8,128)(2,1)}, u32[]{:S(2)}) copy-start(bf16[512,144]{0,1:T(8,128)(2,1)} %param.23) | copy-start | bytes 442372
  199.5 6.4 %collective-permute-start.3 = (bf16[1,16,1,128]{1,3,2,0:T(8,128)(2,1)S(1)}, bf16[1,16,1,128]{1,3,2,0:T(8,128)(2,1)S(1)}, u32[]{:S(2)}, u32[]{:S(2)}) collective-permute-start(bf16[1,16,1,128]{1,3,2,0:T(8,128)(2,1)S(1)} %get-tuple-element.31), channel_id=1, source_target_pairs={{0,1},{1,2},{2,3},{4,5},{5,6},{6,7},{8,9},{9,10},{10,11},{12,13},{... | collective-permute-start | bytes 12296 | tf_op jit(solution)/shard_map/ppermute | solution.py:36
  202.9 5.8 %collective-permute-start.4 = (bf16[1,16,1,128]{1,3,2,0:T(8,128)(2,1)S(1)}, bf16[1,16,1,128]{1,3,2,0:T(8,128)(2,1)S(1)}, u32[]{:S(2)}, u32[]{:S(2)}) collective-permute-start(bf16[1,16,1,128]{1,3,2,0:T(8,128)(2,1)S(1)} %get-tuple-element.32), channel_id=1, source_target_pairs={{1,0},{2,1},{3,2},{5,4},{6,5},{7,6},{9,8},{10,9},{11,10},{13,12},{... | collective-permute-start | bytes 12296 | tf_op jit(solution)/shard_map/ppermute | solution.py:39
Sparse Core Ops, SparseCore 0:
  9.9 51.5 all-gather.4
  67.9 37.0 all-gather.6
  106.6 35.9 all-gather.8
  144.3 29.9 all-gather.10
